TPU v7x, 128 devices: a whole 4x4x4 slice. The times are simulated.
128 devices in a mesh: dp: 16 (over y, x_lo, core), mp: 8 (over x_hi, z).
Axes of the slice: x: 4 (x_hi: 2, x_lo: 2; x = x_hi * 2 + x_lo), y: 4, z: 4, core: 2. Of those that a mesh axis runs over, the one named last changes fastest.
Arguments:
- grads: bfloat16 [256, 2048, 512], P('dp', 'mp'), may hold values from -6 to 6
- old_stat: float32 [256, 512, 512], P(('dp', 'mp')), may hold values from -0.015 to 64, as said below
- counts: int32 [256], P(('dp', 'mp')), may hold values from 2 to 6, as said below
Outputs:
- new_stat: float32 [256, 512, 512], P(('dp', 'mp'))
- roots: bfloat16 [256, 512, 512], P(None, 'mp')
Inputs may be any that keep to these rules, and one draw needn't show every extreme that they name: old_stat is symmetric; each block's diagonal exceeds the sum of magnitudes of its row's other entries. `counts`: at least one block takes 6 iterations.
All inputs are finite; a program needn't handle non-finite values.
Results may differ from a plain program's by a relative error of at most 0.012.
Values may be sent and summed in bfloat16 or wider, within the bound.
A program may use at most 192 MiB of HBM per device.

v0:
```python
import jax
import jax.numpy as jnp
from jax import lax
from jax.sharding import PartitionSpec as P

ITERS = 6


def product(left, right):
    return jnp.einsum(
        "bij,bjk->bik",
        left,
        right,
        preferred_element_type=jnp.float32,
        precision=lax.Precision.HIGHEST,
    )


def newton_step(step, carry, counts, eye):
    mat_m, mat_h = carry
    factor = eye[None] * 1.25 - 0.25 * mat_m
    new_h = product(mat_h, factor)
    square = product(factor, factor)
    fourth = product(square, square)
    new_m = product(fourth, mat_m)
    live = (step < counts)[:, None, None]
    return (jnp.where(live, new_m, mat_m), jnp.where(live, new_h, mat_h))


def body(grads, old_stat, counts):
    order = old_stat.shape[1]
    gram = lax.psum_scatter(
        jnp.einsum("brk,brl->bkl", grads, grads, preferred_element_type=jnp.float32).astype(
            jnp.bfloat16
        ),
        "mp",
        scatter_dimension=0,
        tiled=True,
    ).astype(jnp.float32)
    new_stat = 0.95 * old_stat + 0.05 * gram
    eye = jnp.eye(order, dtype=jnp.float32)
    norm = jnp.sqrt(jnp.sum(new_stat * new_stat, axis=(1, 2)))
    zval = 2.5 / norm
    mat_m = new_stat * zval[:, None, None]
    mat_h = eye[None] * jnp.sqrt(jnp.sqrt(zval))[:, None, None]
    carry = (mat_m, mat_h)
    for step in range(ITERS):
        carry = newton_step(step, carry, counts, eye)
    local_roots = carry[1].astype(jnp.bfloat16)
    slabs = lax.all_to_all(local_roots, "mp", split_axis=1, concat_axis=0, tiled=True)
    roots = lax.all_gather(slabs, "dp", axis=0, tiled=True)
    return (new_stat, roots)


def solution(mesh):
    in_specs = (P("dp", "mp", None), P(("dp", "mp"), None, None), P(("dp", "mp")))
    out_specs = (P(("dp", "mp"), None, None), P(None, "mp", None))
    return jax.shard_map(body, mesh=mesh, in_specs=in_specs, out_specs=out_specs, check_vma=False)
```

profile of v0, /device:TPU:3, one launch (start us, length us, event | category | flops | bytes accessed | tf_op | source)
XLA Modules:
  0.0 347.9 jit_solution(14364567599529328103)
XLA Ops:
  7.2 9.2 %convolution_convert_fusion = bf16[16,512,512]{2,1,0:T(8,128)(2,1)} fusion(bf16[16,256,512]{2,1,0:T(8,128)(2,1)} %param.3), kind=kOutput, calls=%fused_computation | convolution fusion | flops 2151677952 | bytes 12582912 | tf_op jit(solution)/shard_map/brk,brl->bkl/dot_general | solution.py:33
  17.1 115.1 %reduce-scatter.2.cloned.1.call-done = bf16[2,512,512]{2,1,0:T(8,128)(2,1)} async-done(((bf16[16,512,512]{2,1,0:T(8,128)(2,1)}), bf16[2,512,512]{2,1,0:T(8,128)(2,1)}) %reduce-scatter.2.cloned.1.call-update) | async-done | bytes 1048592 | tf_op jit(solution)/shard_map/reduce_scatter | solution.py:32
  134.7 4.0 %fusion.19 = f32[2,512,512]{2,1,0:T(8,128)S(1)} fusion(f32[2,512,512]{2,1,0:T(8,128)S(1)} %get-tuple-element.14, f32[2]{0:T(128)S(1)} %get-tuple-element.11, f32[512,512]{1,0:T(8,128)S(1)} %fusion.47), kind=kOutput, calls=%fused_computation.31 | convolution fusion | flops 3222798336 | bytes 5242888 | tf_op jit(solution)/shard_map/bij,bjk->bik/dot_general | solution.py:10
  138.7 3.5 %fusion.63 = f32[2,512,512]{2,1,0:T(8,128)S(1)} fusion(f32[2,512,512]{2,1,0:T(8,128)S(1)} %fusion.19), kind=kOutput, calls=%fused_computation.84 | convolution fusion | flops 3221225472 | bytes 4194304 | tf_op jit(solution)/shard_map/bij,bjk->bik/dot_general | solution.py:10
  142.2 3.8 %convolution_select_fusion.5 = f32[2,512,512]{2,1,0:T(8,128)S(1)} fusion(f32[2,512,512]{2,1,0:T(8,128)S(1)} %fusion.63, f32[2,512,512]{2,1,0:T(8,128)S(1)} %get-tuple-element.14, f32[2]{0:T(128)S(1)} %get-tuple-element.11, pred[2]{0:T(512)(128)(4,1)S(1)} %get-tuple-element.8), kind=kOutput, calls=%fused_computation.23 | convolution fusion | flops 3222798336 | bytes 6291466 | tf_op jit(solution)/shard_map/bij,bjk->bik/dot_general | solution.py:10
  146.0 4.2 %fusion.11 = f32[2,512,512]{2,1,0:T(8,128)S(1)} fusion(f32[2,512,512]{2,1,0:T(8,128)S(1)} %convolution_select_fusion.5, f32[512,512]{1,0:T(8,128)S(1)} %fusion.47), kind=kOutput, calls=%fused_computation.25 | convolution fusion | flops 3222274048 | bytes 5242880 | tf_op jit(solution)/shard_map/bij,bjk->bik/dot_general | solution.py:10
  153.8 4.0 %multiply_select_fusion = f32[2,512,512]{2,1,0:T(8,128)S(1)} fusion(f32[2,512,512]{2,1,0:T(8,128)S(1)} %get-tuple-element.14, f32[2]{0:T(128)S(1)} %get-tuple-element.11, f32[512,512]{1,0:T(8,128)S(1)} %fusion.47, f32[2]{0:T(128)S(1)} %get-tuple-element.10, f32[512,512]{1,0:T(8,128)S(1)} %fusion.48, pred[2]{0:T(512)(128)(4,1)S(1)} %get-tuple-element.8), kind=kOutput, calls=%fused_computation.1 | convolution fusion | flops 3224371200 | bytes 6291474 | tf_op jit(solution)/shard_map/bij,bjk->bik/dot_general | solution.py:10
  157.8 3.7 %fusion.12 = f32[2,512,512]{2,1,0:T(8,128)S(1)} fusion(f32[2,512,512]{2,1,0:T(8,128)S(1)} %multiply_select_fusion, f32[2,512,512]{2,1,0:T(8,128)S(1)} %convolution_select_fusion.5, f32[512,512]{1,0:T(8,128)S(1)} %fusion.47), kind=kOutput, calls=%fused_computation.26 | convolution fusion | flops 3222274048 | bytes 7340032 | tf_op jit(solution)/shard_map/bij,bjk->bik/dot_general | solution.py:10
  161.5 3.8 %convolution_select_fusion.4 = f32[2,512,512]{2,1,0:T(8,128)S(1)} fusion(f32[2,512,512]{2,1,0:T(8,128)S(1)} %convolution_select_fusion.5, f32[2,512,512]{2,1,0:T(8,128)S(1)} %fusion.64, pred[2]{0:T(512)(128)(4,1)S(1)} %get-tuple-element.9), kind=kOutput, calls=%fused_computation.22 | convolution fusion | flops 3221749760 | bytes 6291458 | tf_op jit(solution)/shard_map/bij,bjk->bik/dot_general | solution.py:10
  165.3 3.7 %fusion.13 = f32[2,512,512]{2,1,0:T(8,128)S(1)} fusion(f32[2,512,512]{2,1,0:T(8,128)S(1)} %convolution_select_fusion.4, f32[512,512]{1,0:T(8,128)S(1)} %fusion.47), kind=kOutput, calls=%fused_computation.27 | convolution fusion | flops 3222274048 | bytes 5242880 | tf_op jit(solution)/shard_map/bij,bjk->bik/dot_general | solution.py:10
  169.0 3.5 %fusion.65 = f32[2,512,512]{2,1,0:T(8,128)S(1)} fusion(f32[2,512,512]{2,1,0:T(8,128)S(1)} %fusion.13), kind=kOutput, calls=%fused_computation.86 | convolution fusion | flops 3221225472 | bytes 4194304 | tf_op jit(solution)/shard_map/bij,bjk->bik/dot_general | solution.py:10
  172.6 3.9 %convolution_select_fusion.3 = f32[2,512,512]{2,1,0:T(8,128)S(1)} fusion(f32[2,512,512]{2,1,0:T(8,128)S(1)} %fusion.12, f32[2,512,512]{2,1,0:T(8,128)S(1)} %multiply_select_fusion, f32[2,512,512]{2,1,0:T(8,128)S(1)} %convolution_select_fusion.4, f32[512,512]{1,0:T(8,128)S(1)} %fusion.47, pred[2]{0:T(512)(128)(4,1)S(1)} %get-tuple-element.9, ...), kind=kOutput, calls=%fused_computation.20 | convolution fusion | flops 3223846912 | bytes 9437188 | tf_op jit(solution)/shard_map/bij,bjk->bik/dot_general | solution.py:10
  176.5 3.8 %convolution_select_fusion.2 = f32[2,512,512]{2,1,0:T(8,128)S(1)} fusion(f32[2,512,512]{2,1,0:T(8,128)S(1)} %convolution_select_fusion.4, f32[2,512,512]{2,1,0:T(8,128)S(1)} %fusion.65, pred[2]{0:T(512)(128)(4,1)S(1)} %get-tuple-element.5), kind=kOutput, calls=%fused_computation.19 | convolution fusion | flops 3221749760 | bytes 6291458 | tf_op jit(solution)/shard_map/bij,bjk->bik/dot_general | solution.py:10
  180.3 3.7 %fusion.14 = f32[2,512,512]{2,1,0:T(8,128)S(1)} fusion(f32[2,512,512]{2,1,0:T(8,128)S(1)} %convolution_select_fusion.2, f32[512,512]{1,0:T(8,128)S(1)} %fusion.47), kind=kOutput, calls=%fused_computation.28 | convolution fusion | flops 3222274048 | bytes 5242880 | tf_op jit(solution)/shard_map/bij,bjk->bik/dot_general | solution.py:10
  184.0 3.5 %fusion.66 = f32[2,512,512]{2,1,0:T(8,128)S(1)} fusion(f32[2,512,512]{2,1,0:T(8,128)S(1)} %fusion.14), kind=kOutput, calls=%fused_computation.87 | convolution fusion | flops 3221225472 | bytes 4194304 | tf_op jit(solution)/shard_map/bij,bjk->bik/dot_general | solution.py:10
  187.5 4.1 %fusion.15 = f32[2,512,512]{2,1,0:T(8,128)S(1)} fusion(f32[2,512,512]{2,1,0:T(8,128)S(1)} %convolution_select_fusion.3, f32[2,512,512]{2,1,0:T(8,128)S(1)} %convolution_select_fusion.2, f32[512,512]{1,0:T(8,128)S(1)} %fusion.47), kind=kOutput, calls=%fused_computation.29 | convolution fusion | flops 3222274048 | bytes 7340032 | tf_op jit(solution)/shard_map/bij,bjk->bik/dot_general | solution.py:10
  191.6 3.6 %convolution_select_fusion.1 = f32[2,512,512]{2,1,0:T(8,128)S(1)} fusion(f32[2,512,512]{2,1,0:T(8,128)S(1)} %convolution_select_fusion.2, f32[2,512,512]{2,1,0:T(8,128)S(1)} %fusion.66, pred[2]{0:T(512)(128)(4,1)S(1)} %get-tuple-element.6), kind=kOutput, calls=%fused_computation.18 | convolution fusion | flops 3221749760 | bytes 6291458 | tf_op jit(solution)/shard_map/bij,bjk->bik/dot_general | solution.py:10
  195.2 3.7 %fusion.16 = f32[2,512,512]{2,1,0:T(8,128)S(1)} fusion(f32[2,512,512]{2,1,0:T(8,128)S(1)} %convolution_select_fusion.1, f32[512,512]{1,0:T(8,128)S(1)} %fusion.47), kind=kOutput, calls=%fused_computation.30 | convolution fusion | flops 3222274048 | bytes 5242880 | tf_op jit(solution)/shard_map/bij,bjk->bik/dot_general | solution.py:10
  202.5 3.7 %fusion.68 = f32[2,512,512]{2,1,0:T(8,128)S(1)} fusion(f32[2,512,512]{2,1,0:T(8,128)S(1)} %fusion.67, f32[2,512,512]{2,1,0:T(8,128)S(1)} %convolution_select_fusion.1), kind=kOutput, calls=%fused_computation.89 | convolution fusion | flops 3221225472 | bytes 6291456 | tf_op jit(solution)/shard_map/bij,bjk->bik/dot_general | solution.py:10
  206.2 3.9 %convolution_select_fusion = f32[2,512,512]{2,1,0:T(8,128)S(1)} fusion(f32[2,512,512]{2,1,0:T(8,128)S(1)} %fusion.15, f32[2,512,512]{2,1,0:T(8,128)S(1)} %convolution_select_fusion.3, f32[2,512,512]{2,1,0:T(8,128)S(1)} %convolution_select_fusion.1, f32[512,512]{1,0:T(8,128)S(1)} %fusion.47, pred[2]{0:T(512)(128)(4,1)S(1)} %get-tuple-element.6, ...), kind=kOutput, calls=%fused_computation.16 | convolution fusion | flops 3223846912 | bytes 9437188 | tf_op jit(solution)/shard_map/bij,bjk->bik/dot_general | solution.py:10
  210.1 4.0 %select_convert_fusion = bf16[2,512,512]{2,1,0:T(8,128)(2,1)S(1)} fusion(f32[2,512,512]{2,1,0:T(8,128)S(1)} %convolution_select_fusion, f32[2,512,512]{2,1,0:T(8,128)S(1)} %fusion.68, f32[2,512,512]{2,1,0:T(8,128)S(1)} %convolution_select_fusion.1, f32[512,512]{1,0:T(8,128)S(1)} %fusion.47, pred[2]{0:T(512)(128)(4,1)S(1)} %get-tuple-element.7, ...), kind=kOutput, calls=%fused_computation.4 | convolution fusion | flops 3223846912 | bytes 8388612 | tf_op jit(solution)/shard_map/bij,bjk->bik/dot_general | solution.py:10
  215.2 17.8 %all_to_all.18 = bf16[2,512,512]{2,0,1:T(2,128)(2,1)S(1)} all-to-all(bf16[2,512,512]{2,0,1:T(2,128)(2,1)S(1)} %copy.8), channel_id=1, replica_groups=mesh['dp'=16,'mp'=8] {'mp'}, dimensions={1} | all-to-all | bytes 2097152 | tf_op jit(solution)/shard_map/all_to_all | solution.py:50
  234.3 92.6 %all-gather.2.cloned.1.call-done = bf16[256,64,512]{2,1,0:T(8,128)(2,1)} async-done(((bf16[16,64,512]{2,1,0:T(8,128)(2,1)}), bf16[256,64,512]{2,1,0:T(8,128)(2,1)}) %all-gather.2.cloned.1.call-update) | async-done | bytes 16777232 | tf_op jit(solution)/shard_map/all_gather | solution.py:51
  326.8 14.1 %copy.12 = bf16[256,64,512]{2,1,0:T(8,128)(2,1)} copy(bf16[256,64,512]{2,1,0:T(8,128)(2,1)} %all-gather.2.cloned.1.call-done) | data formatting | bytes 33554432
  (17 shorter events, 12.5 us)
Async XLA Ops:
  7.2 125.0 %reduce-scatter.2.cloned.1.call-start = ((), (), s32[]{:S(2)}) async-start(), calls=%async_computation.2 | async-start | bytes 9437184 | tf_op jit(solution)/shard_map/reduce_scatter | solution.py:32
  16.5 0.7 copy-start.1
  16.5 310.3 %all-gather.2.cloned.1.call-start = ((), (), s32[]{:S(2)}) async-start(), calls=%async_computation.3 | async-start | bytes 17825792 | tf_op jit(solution)/shard_map/all_gather | solution.py:51
  134.7 19.1 %copy-start = (f32[2,512,512]{2,1,0:T(8,128)}, f32[2,512,512]{2,1,0:T(8,128)S(1)}, u32[]{:S(2)}) copy-start(f32[2,512,512]{2,1,0:T(8,128)S(1)} %get-tuple-element.14) | copy-start | bytes 6291460
Sparse Core Ops, SparseCore 0:
  16.6 115.5 reduce-scatter.1
  234.4 92.3 all-gather.1
where the time goes:
time: 352 us; the launch traced here: 348 us
  waiting for transfers between devices  208 us (59%)
  matrix products  88.5 us (25%)
  blocking collectives  17.8 us (5%)
  local copies, waits for them, and re-layouts  16.4 us (5%)
  between operations  14.4 us (4%)
    reduce_scatter x1, waiting for transfers between devices, body(): lax.psum_scatter(jnp.einsum('brk,brl->bkl', grads, grads, preferred_eleme...  115 us
    all_gather x1, waiting for transfers between devices, body(): roots = lax.all_gather(slabs, 'dp', axis=0, tiled=True)  92.6 us
    dot_general x21, matrix products, product(): jnp.einsum('bij,bjk->bik', left, right, preferred_element_type=jnp.float3...  79.3 us
    all_to_all x1, blocking collectives, body(): lax.all_to_all(local_roots, 'mp', split_axis=1, concat_axis=0, tiled=True)  17.8 us
    unnamed x5, local copies, waits for them, and re-layouts  14.1 us
    dot_general x1, matrix products, body(): jnp.einsum('brk,brl->bkl', grads, grads, preferred_element_type=jnp.float32)  9.25 us
  transfers between devices with their start and end apart: 2, of which 2 were waited for; matrix products, arithmetic and copies ran while one was open for 0% of the time, Pallas kernels for 0%

commit v1 on v0

v1 whole, which is shorter than its diff:
```python
import functools

import jax
import jax.numpy as jnp
from jax import lax
from jax.experimental import pallas as pl
from jax.experimental.pallas import tpu as pltpu
from jax.sharding import PartitionSpec as P

MESH = pl.DeviceIdType.MESH
F32, BF16 = jnp.float32, jnp.bfloat16
ITERS = 6
NY, NX, NC, NP = 4, 2, 2, 8
C0, C1, C2, C3, C4 = 1.25**4, -4 * 1.25**3 * 0.25, 6 * 1.25**2 * 0.25**2, -4 * 1.25 * 0.25**3, 0.25**4


def dot(left, right):
    return jnp.dot(left, right, preferred_element_type=F32)


def kernel(grads, old_hbm, counts, stat, out, got, old, root, mat, mat_b, sq_b, mix_b, mat_h, acc, sems):
    order = old.shape[1]
    dp, mp = lax.axis_index("dp"), lax.axis_index("mp")
    rows = grads.shape[1]
    slab = order // NP
    chunk = order // 2
    parts = [slice(r, r + chunk) for r in range(0, order, chunk)]

    across = (dp ^ 2, mp)
    up = (lax.rem(dp + 4, NY * NX * NC), mp)
    down = (lax.rem(dp + 12, NY * NX * NC), mp)
    sibling = (dp ^ 1, mp)
    peers = [(dp, mp ^ p) for p in range(NP)]

    barrier = pltpu.get_barrier_semaphore()
    partners = peers[1:] + [across, up, down, sibling]
    for partner in partners:
        pl.semaphore_signal(barrier, inc=1, device_id=partner, device_id_type=MESH)

    keep = [pltpu.make_async_copy(old_hbm.at[j], old.at[j], sems["old"].at[j]) for j in range(2)]
    for copy in keep:
        copy.start()
    mine = [
        pltpu.make_async_copy(
            grads.at[2 * mp + j], got.at[j, pl.ds(mp * rows, rows)], sems["mine"].at[j]
        )
        for j in range(2)
    ]
    for copy in mine:
        copy.start()
    pl.semaphore_wait(barrier, len(partners))

    def grad_copy(j, p):
        return pltpu.make_async_remote_copy(
            src_ref=grads.at[2 * (mp ^ p) + j],
            dst_ref=got.at[j, pl.ds(mp * rows, rows)],
            send_sem=sems["gsend"].at[j, p],
            recv_sem=sems["grecv"].at[j, p],
            device_id=peers[p],
            device_id_type=MESH,
        )

    grad_copies = [[p and grad_copy(j, p) for p in range(NP)] for j in range(2)]

    def add_gram(j, p):
        block = got[j, pl.ds(pl.multiple_of((mp ^ p) * rows, rows), rows), :]
        gram = lax.dot_general(block, block, (((0,), (0,)), ((), ())), preferred_element_type=F32)
        if p == 0:
            acc[...] = gram
        else:
            acc[...] += gram

    def update_stat(j):
        keep[j].wait()
        total = jnp.zeros((1, order), F32)
        for r in parts:
            new = 0.95 * old[j, r, :] + 0.05 * acc[r, :]
            stat[j, r, :] = new
            total = total + jnp.sum(new * new, axis=0, keepdims=True)
        total = jnp.sum(total, axis=1, keepdims=True)
        zval = 2.5 / jnp.sqrt(total)
        start = jnp.sqrt(jnp.sqrt(zval))
        for r in parts:
            scaled = stat[j, r, :] * zval
            mat[r, :] = scaled
            mat_b[r, :] = scaled.astype(BF16)
            row = lax.broadcasted_iota(jnp.int32, (chunk, order), 0) + r.start
            col = lax.broadcasted_iota(jnp.int32, (chunk, order), 1)
            mat_h[r, :] = start * (jnp.where(row == col, 1.25, 0.0) - 0.25 * scaled)

    def step_m():
        for r in parts:
            square = dot(mat_b[r, :], mat_b[...])
            sq_b[r, :] = square.astype(BF16)
            mat[r, :] = C0 * mat[r, :] + C1 * square
        for r in parts:
            cube = dot(mat_b[r, :], sq_b[...])
            mat[r, :] = mat[r, :] + C2 * cube
            mix_b[r, :] = (C3 * sq_b[r, :].astype(F32) + C4 * cube).astype(BF16)
        for r in parts:
            new = mat[r, :] + dot(sq_b[r, :], mix_b[...])
            mat[r, :] = new
            mat_b[r, :] = new.astype(BF16)

    def step_h(j, it):
        share = jnp.where(it < counts[j], 0.25, 0.0).astype(F32)
        for r in parts:
            held = mat_h[r, :]
            mat_h[r, :] = held + share * (held - dot(held.astype(BF16), mat_b[...]))

    def finish(j):
        share = jnp.where(ITERS - 1 < counts[j], 0.25, 0.0).astype(F32)
        for r in parts:
            held = mat_h[r, :]
            held = held + share * (held - dot(held.astype(BF16), mat_b[...]))
            root[j, r, :] = held.astype(BF16)

    def slab_copy(j, p):
        return pltpu.make_async_remote_copy(
            src_ref=root.at[j, pl.ds(pl.multiple_of((mp ^ p) * slab, slab), slab)],
            dst_ref=out.at[dp, mp, j],
            send_sem=sems["ssend"].at[j, p],
            recv_sem=sems["srecv"].at[j, p],
            device_id=peers[p],
            device_id_type=MESH,
        )

    slab_copies = [[p and slab_copy(j, p) for p in range(NP)] for j in range(2)]

    def piece(j, dy, dx, t):
        origin = lax.rem(dp + 4 * (NY - dy), NY * NX * NC) ^ (2 * dx)
        return out.at[origin, pl.ds(2 * ((mp // 2) ^ t), 2), j]

    def move(j, dy, dx, t, way):
        target = {"x": across, "+": up, "-": down, "s": sibling}[way]
        to_dy = {"x": dy, "+": (dy + 1) % NY, "-": (dy - 1) % NY, "s": dy}[way]
        to_dx = dx ^ 1 if way == "x" else dx
        side = "xys"["x+-s".index(way) if way == "x" else (2 if way == "s" else 1)]
        name = {"x": 0, "y": 0, "s": 1}[side]
        return pltpu.make_async_remote_copy(
            src_ref=piece(j, dy, dx, t),
            dst_ref=piece(j, dy, dx, t),
            send_sem=sems["bsend"].at[j, "x+-s".index(way), dy * 2 + dx, t],
            recv_sem=sems["brecv"].at[j, name, to_dy * 2 + to_dx, t],
            device_id=target,
            device_id_type=MESH,
        )

    started = []

    def send(j, dy, dx, t, ways):
        for way in ways:
            copy = move(j, dy, dx, t, way)
            copy.start()
            started.append(copy)

    def arrived(j, dy, dx, t, side=0):
        pltpu.make_async_remote_copy(
            src_ref=piece(j, dy, dx, t),
            dst_ref=piece(j, dy, dx, t),
            send_sem=sems["bsend"].at[j, 3, dy * 2 + dx, t],
            recv_sem=sems["brecv"].at[j, side, dy * 2 + dx, t],
            device_id=sibling,
            device_id_type=MESH,
        ).wait_recv()

    def spread(j):
        for p in range(1, NP):
            slab_copies[j][p].start()
        out[dp, mp, j] = root[j, pl.ds(pl.multiple_of(mp * slab, slab), slab), :]
        for t in range(NP // 2):
            for p in (2 * t, 2 * t + 1):
                if p:
                    slab_copies[j][p].wait_recv()
            send(j, 0, 0, t, {0: "x+-s", 1: "x-+s", 2: "+-xs", 3: "-+xs"}[t])

    relays = [
        (0, 1, 0, "+-s"),
        (0, 1, 1, "-+s"),
        (1, 0, 0, "+s"),
        (3, 0, 1, "-s"),
        (1, 0, 2, "+xs"),
        (3, 0, 3, "-xs"),
        (3, 0, 2, "xs"),
        (1, 0, 3, "xs"),
        (1, 0, 1, "s"),
        (3, 0, 0, "s"),
        (0, 1, 2, "s"),
        (0, 1, 3, "s"),
        (1, 1, 0, "+s"),
        (3, 1, 1, "-s"),
        (1, 1, 1, "s"),
        (3, 1, 0, "s"),
        (2, 0, 2, "xs"),
        (2, 0, 3, "xs"),
        (2, 0, 0, "s"),
        (2, 0, 1, "s"),
        (1, 1, 2, "s"),
        (3, 1, 3, "s"),
        (3, 1, 2, "s"),
        (1, 1, 3, "s"),
        (2, 1, 0, "s"),
        (2, 1, 1, "s"),
        (2, 1, 2, "s"),
        (2, 1, 3, "s"),
    ]

    def relay(j, first, last):
        for dy, dx, t, ways in relays[first:last]:
            arrived(j, dy, dx, t)
            send(j, dy, dx, t, ways)

    for p in range(1, NP):
        grad_copies[0][p].start()
    mine[0].wait()
    add_gram(0, 0)
    for p in range(1, NP):
        grad_copies[0][p].wait_recv()
        add_gram(0, p)
        grad_copies[0][p].wait_send()
        grad_copies[1][p].start()
    update_stat(0)
    step_m()

    def body(it, _):
        step_h(0, it)
        step_m()
        return 0

    lax.fori_loop(1, ITERS - 1, body, 0)
    finish(0)
    spread(0)

    mine[1].wait()
    add_gram(1, 0)
    relay(0, 0, 2)
    for p in range(1, NP):
        grad_copies[1][p].wait_recv()
        add_gram(1, p)
        grad_copies[1][p].wait_send()
    update_stat(1)
    step_m()
    relay(0, 2, 4)
    stops = {1: (4, 8), 2: (8, 12), 3: (12, 16), 4: (16, 20)}
    for it in range(1, ITERS - 1):
        step_h(1, it)
        step_m()
        relay(0, *stops[it])
    finish(1)
    spread(1)
    relay(0, 20, len(relays))
    relay(1, 0, len(relays))

    for j in range(2):
        for dy in range(NY):
            for dx in range(NX):
                for t in range(4):
                    arrived(j, dy, dx, t, 1)
        for p in range(1, NP):
            slab_copies[j][p].wait_send()
    for copy in started:
        copy.wait_send()


def solution(mesh):
    def step(grads, old_stat, counts):
        order = old_stat.shape[1]
        rows = grads.shape[1]
        slab = order // NP
        square = (order, order)
        anywhere = pl.BlockSpec(memory_space=pl.ANY)
        sems = {
            "old": pltpu.SemaphoreType.DMA((2,)),
            "mine": pltpu.SemaphoreType.DMA((2,)),
            "gsend": pltpu.SemaphoreType.DMA((2, NP)),
            "grecv": pltpu.SemaphoreType.DMA((2, NP)),
            "ssend": pltpu.SemaphoreType.DMA((2, NP)),
            "srecv": pltpu.SemaphoreType.DMA((2, NP)),
            "bsend": pltpu.SemaphoreType.DMA((2, 4, NY * NX, 4)),
            "brecv": pltpu.SemaphoreType.DMA((2, 2, NY * NX, 4)),
        }
        stat, out = pl.pallas_call(
            kernel,
            out_shape=(
                pltpu.VMEM((2, order, order), F32),
                pltpu.VMEM((NY * NX * NC, NP, 2, slab, order), BF16),
            ),
            in_specs=[anywhere, anywhere, pl.BlockSpec(memory_space=pltpu.SMEM)],
            out_specs=(pl.BlockSpec(memory_space=pltpu.VMEM), pl.BlockSpec(memory_space=pltpu.VMEM)),
            scratch_shapes=[
                pltpu.VMEM((2, NP * rows, order), BF16),
                pltpu.VMEM((2, order, order), F32),
                pltpu.VMEM((2, order, order), BF16),
                pltpu.VMEM(square, F32),
                pltpu.VMEM(square, BF16),
                pltpu.VMEM(square, BF16),
                pltpu.VMEM(square, BF16),
                pltpu.VMEM(square, F32),
                pltpu.VMEM(square, F32),
                sems,
            ],
            name="shampoo_roots",
            compiler_params=pltpu.CompilerParams(
                collective_id=0, has_side_effects=True, vmem_limit_bytes=24 * 2**20
            ),
        )(grads, old_stat, counts)
        return stat, out.reshape(NY * NX * NC * NP * 2, slab, order)

    return jax.shard_map(
        step,
        mesh=mesh,
        in_specs=(P("dp", "mp", None), P(("dp", "mp"), None, None), P(("dp", "mp"))),
        out_specs=(P(("dp", "mp"), None, None), P(None, "mp", None)),
        check_vma=False,
    )
```

time: 352 us -> 149 us (0.42); the launches traced: 348 us -> 149 us
  waiting for transfers between devices: 208 us -> 0 us
  Pallas kernels: 0 us -> 136 us
  matrix products: 88.5 us -> 0 us
  blocking collectives: 17.8 us -> 0 us
  between operations: 14.4 us -> 0.65 us
  local copies, waits for them, and re-layouts: 16.4 us -> 11.9 us
    pallas_call x0 -> x1, Pallas kernels: none -> 136 us  [step(): pl.pallas_call(kernel, out_shape=(pltpu.VMEM((2, order, order), F32), plt...]
    reduce_scatter x1 -> x0, waiting for transfers between devices: 115 us -> none  [body(): lax.psum_scatter(jnp.einsum('brk,brl->bkl', grads, grads, preferred_eleme...]
    all_gather x1 -> x0, waiting for transfers between devices: 92.6 us -> none  [body(): roots = lax.all_gather(slabs, 'dp', axis=0, tiled=True)]
    dot_general x22 -> x0, matrix products: 88.5 us -> none  [the longest x21 79.3 us: product(): jnp.einsum('bij,bjk->bik', left, right, preferred_element_type=jnp.float3...]
    all_to_all x1 -> x0, blocking collectives: 17.8 us -> none  [body(): lax.all_to_all(local_roots, 'mp', split_axis=1, concat_axis=0, tiled=True)]
    unnamed x5 -> x8, local copies, waits for them, and re-layouts: 14.1 us -> 11.9 us
  transfers between devices with their start and end apart: 2 -> 0, of which waited for: 2 -> 0; matrix products, arithmetic and copies ran while one was open for 0% -> 0% of each run, Pallas kernels for 0% -> 0%
where the time goes in v1:
time: 149 us
  Pallas kernels  136 us (91%)
  local copies, waits for them, and re-layouts  11.9 us (8%)
    pallas_call x1, Pallas kernels, step(): pl.pallas_call(kernel, out_shape=(pltpu.VMEM((2, order, order), F32), plt...  136 us
    unnamed x8, local copies, waits for them, and re-layouts  11.9 us

profile of v1, /device:TPU:3, one launch (start us, length us, event | category | flops | bytes accessed | tf_op | source)
XLA Modules:
  0.0 148.6 jit_solution(16128048298323801139)
XLA Ops:
  0.6 0.0 copy-start
  0.6 2.2 %copy-done = bf16[16,256,512]{2,1,0:T(8,128)(2,1)S(1)} copy-done((bf16[16,256,512]{2,1,0:T(8,128)(2,1)S(1)}, bf16[16,256,512]{2,1,0:T(8,128)(2,1)}, u32[]{:S(2)}) %copy-start) | copy-done | bytes 4194328
  2.8 0.0 copy-start.1
  2.8 1.6 %copy-done.1 = f32[2,512,512]{2,1,0:T(8,128)S(1)} copy-done((f32[2,512,512]{2,1,0:T(8,128)S(1)}, f32[2,512,512]{2,1,0:T(8,128)}, u32[]{:S(2)}) %copy-start.1) | copy-done | bytes 2097176
  4.4 0.0 copy-start.2
  4.4 0.7 copy-done.2
  5.1 136.0 %shampoo_roots.1 = (f32[2,512,512]{2,1,0:T(8,128)S(1)}, bf16[16,8,2,64,512]{4,3,2,1,0:T(8,128)(2,1)S(1)}) custom-call(bf16[16,256,512]{2,1,0:T(8,128)(2,1)S(1)} %copy-done, f32[2,512,512]{2,1,0:T(8,128)S(1)} %copy-done.1, s32[2]{0:T(128)S(1)} %copy-done.2), custom_call_target="tpu_custom_call" | custom-call | tf_op jit(solution)/shard_map/shampoo_roots/pallas_call | solution.py:282
  141.1 1.3 copy.7
  142.4 6.2 %copy.8 = bf16[256,64,512]{2,1,0:T(8,128)(2,1)} copy(bf16[256,64,512]{2,1,0:T(8,128)(2,1)S(1)} %bitcast.1) | data formatting | bytes 33554432
Async XLA Ops:
  0.6 2.2 %copy-start = (bf16[16,256,512]{2,1,0:T(8,128)(2,1)S(1)}, bf16[16,256,512]{2,1,0:T(8,128)(2,1)}, u32[]{:S(2)}) copy-start(bf16[16,256,512]{2,1,0:T(8,128)(2,1)} %grads.1) | copy-start | bytes 12582916
  2.8 1.6 %copy-start.1 = (f32[2,512,512]{2,1,0:T(8,128)S(1)}, f32[2,512,512]{2,1,0:T(8,128)}, u32[]{:S(2)}) copy-start(f32[2,512,512]{2,1,0:T(8,128)} %old_hbm.1) | copy-start | bytes 6291460
  4.4 0.7 copy-start.2

commit v2 on v1

--- a/solution.py
+++ b/solution.py
@@ -14,11 +14,51 @@
 C0, C1, C2, C3, C4 = 1.25**4, -4 * 1.25**3 * 0.25, 6 * 1.25**2 * 0.25**2, -4 * 1.25 * 0.25**3, 0.25**4
 
 
+STORES = 8
+X, Y = "x", "y"
+MOST = ((X, "-"), (X, "+"), (X, "-"), (Y, "+"))
+HALF = ((X, "+"), (X, "-"), (Y, "+"), (Y, "-"))
+KINDS = (MOST, HALF)
+STOPS = (4, 12, 15, 18, 21, 24, 28)
+
+
+def ways_on(kind, dy, dx):
+    first, far = kind
+    near = "-" if far == "+" else "+"
+    ways = ""
+    if first == "x" and (dy, dx) == (0, 0):
+        ways += "x"
+    if first == "x" or dx == 0:
+        if dy == 0:
+            ways += far + near
+        elif dy == (1 if far == "+" else NY - 1):
+            ways += far
+    if first == "y" and dx == 0:
+        ways += "x"
+    return ways
+
+
+def arrival_order(kinds):
+    free = {"x": 0.0, "+": 0.0, "-": 0.0}
+    events = [(0.6 * t, 0, 0, t) for t in range(len(kinds))]
+    order = []
+    while events:
+        events.sort()
+        now, dy, dx, t = events.pop(0)
+        if (dy, dx) != (0, 0):
+            order.append((dy, dx, t))
+        for way in ways_on(kinds[t], dy, dx):
+            free[way] = max(free[way], now) + 1.0
+            to_dy = (dy + {"x": 0, "+": 1, "-": -1}[way]) % NY
+            events.append((free[way] + 1.0, to_dy, dx ^ 1 if way == "x" else dx, t))
+    return order
+
+
 def dot(left, right):
     return jnp.dot(left, right, preferred_element_type=F32)
 
 
-def kernel(grads, old_hbm, counts, stat, out, got, old, root, mat, mat_b, sq_b, mix_b, mat_h, acc, sems):
+def kernel(grads, old_hbm, counts_hbm, stat, out, counts, got, old, root, mat, mat_b, sq_b, mix_b, mat_h, acc, sems):
     order = old.shape[1]
     dp, mp = lax.axis_index("dp"), lax.axis_index("mp")
     rows = grads.shape[1]
@@ -38,6 +78,8 @@
         pl.semaphore_signal(barrier, inc=1, device_id=partner, device_id_type=MESH)
 
     keep = [pltpu.make_async_copy(old_hbm.at[j], old.at[j], sems["old"].at[j]) for j in range(2)]
+    tally = pltpu.make_async_copy(counts_hbm, counts, sems["count"])
+    tally.start()
     for copy in keep:
         copy.start()
     mine = [
@@ -172,53 +214,35 @@
             for p in (2 * t, 2 * t + 1):
                 if p:
                     slab_copies[j][p].wait_recv()
-            send(j, 0, 0, t, {0: "x+-s", 1: "x-+s", 2: "+-xs", 3: "-+xs"}[t])
-
-    relays = [
-        (0, 1, 0, "+-s"),
-        (0, 1, 1, "-+s"),
-        (1, 0, 0, "+s"),
-        (3, 0, 1, "-s"),
-        (1, 0, 2, "+xs"),
-        (3, 0, 3, "-xs"),
-        (3, 0, 2, "xs"),
-        (1, 0, 3, "xs"),
-        (1, 0, 1, "s"),
-        (3, 0, 0, "s"),
-        (0, 1, 2, "s"),
-        (0, 1, 3, "s"),
-        (1, 1, 0, "+s"),
-        (3, 1, 1, "-s"),
-        (1, 1, 1, "s"),
-        (3, 1, 0, "s"),
-        (2, 0, 2, "xs"),
-        (2, 0, 3, "xs"),
-        (2, 0, 0, "s"),
-        (2, 0, 1, "s"),
-        (1, 1, 2, "s"),
-        (3, 1, 3, "s"),
-        (3, 1, 2, "s"),
-        (1, 1, 3, "s"),
-        (2, 1, 0, "s"),
-        (2, 1, 1, "s"),
-        (2, 1, 2, "s"),
-        (2, 1, 3, "s"),
-    ]
+            send(j, 0, 0, t, ways_on(KINDS[j][t], 0, 0) + "s")
+
+    relays = [arrival_order(KINDS[j]) for j in range(2)]
 
     def relay(j, first, last):
-        for dy, dx, t, ways in relays[first:last]:
+        for dy, dx, t in relays[j][first:last]:
             arrived(j, dy, dx, t)
-            send(j, dy, dx, t, ways)
-
-    for p in range(1, NP):
+            send(j, dy, dx, t, ways_on(KINDS[j][t], dy, dx) + "s")
+
+    core = lax.rem(dp, NC)
+
+    def take_turn(p):
+        pl.semaphore_wait(sems["turn"].at[p], 1)
+
+    def pass_turn(p):
+        pl.semaphore_signal(sems["turn"].at[p], inc=1, device_id=sibling, device_id_type=MESH)
+
+    for p in range(1, NP):
+        pl.when(core == 1)(functools.partial(take_turn, p))
         grad_copies[0][p].start()
     mine[0].wait()
     add_gram(0, 0)
     for p in range(1, NP):
+        grad_copies[0][p].wait_send()
+        pass_turn(p)
+    for p in range(1, NP):
         grad_copies[0][p].wait_recv()
         add_gram(0, p)
-        grad_copies[0][p].wait_send()
-        grad_copies[1][p].start()
+    tally.wait()
     update_stat(0)
     step_m()
 
@@ -229,27 +253,32 @@
 
     lax.fori_loop(1, ITERS - 1, body, 0)
     finish(0)
+
     spread(0)
-
+    for p in range(1, NP):
+        pl.when(core == 0)(functools.partial(take_turn, p))
+        grad_copies[1][p].start()
+
+    relay(0, 0, STOPS[0])
+    relay(0, STOPS[0], STOPS[1])
     mine[1].wait()
     add_gram(1, 0)
-    relay(0, 0, 2)
+    for p in range(1, NP):
+        grad_copies[1][p].wait_send()
     for p in range(1, NP):
         grad_copies[1][p].wait_recv()
         add_gram(1, p)
-        grad_copies[1][p].wait_send()
     update_stat(1)
     step_m()
-    relay(0, 2, 4)
-    stops = {1: (4, 8), 2: (8, 12), 3: (12, 16), 4: (16, 20)}
     for it in range(1, ITERS - 1):
+        relay(0, STOPS[it], STOPS[it + 1])
         step_h(1, it)
         step_m()
-        relay(0, *stops[it])
+    relay(0, STOPS[ITERS - 1], STOPS[ITERS])
     finish(1)
     spread(1)
-    relay(0, 20, len(relays))
-    relay(1, 0, len(relays))
+    relay(0, STOPS[ITERS], len(relays[0]))
+    relay(1, 0, len(relays[1]))
 
     for j in range(2):
         for dy in range(NY):
@@ -262,16 +291,29 @@
         copy.wait_send()
 
 
+def store(stat, out, stat_to, out_to, sems):
+    size = out.shape[0] // STORES
+    copies = [pltpu.make_async_copy(stat, stat_to, sems.at[STORES])]
+    for k in range(STORES):
+        span = pl.ds(k * size, size)
+        copies.append(pltpu.make_async_copy(out.at[span], out_to.at[span], sems.at[k]))
+    for copy in copies:
+        copy.start()
+    for copy in copies:
+        copy.wait()
+
+
 def solution(mesh):
     def step(grads, old_stat, counts):
         order = old_stat.shape[1]
         rows = grads.shape[1]
         slab = order // NP
         square = (order, order)
-        anywhere = pl.BlockSpec(memory_space=pl.ANY)
         sems = {
             "old": pltpu.SemaphoreType.DMA((2,)),
             "mine": pltpu.SemaphoreType.DMA((2,)),
+            "count": pltpu.SemaphoreType.DMA(()),
+            "turn": pltpu.SemaphoreType.REGULAR((NP,)),
             "gsend": pltpu.SemaphoreType.DMA((2, NP)),
             "grecv": pltpu.SemaphoreType.DMA((2, NP)),
             "ssend": pltpu.SemaphoreType.DMA((2, NP)),
@@ -285,9 +327,10 @@
                 pltpu.VMEM((2, order, order), F32),
                 pltpu.VMEM((NY * NX * NC, NP, 2, slab, order), BF16),
             ),
-            in_specs=[anywhere, anywhere, pl.BlockSpec(memory_space=pltpu.SMEM)],
+            in_specs=[pl.BlockSpec(memory_space=pltpu.HBM)] * 3,
             out_specs=(pl.BlockSpec(memory_space=pltpu.VMEM), pl.BlockSpec(memory_space=pltpu.VMEM)),
             scratch_shapes=[
+                pltpu.SMEM((2,), jnp.int32),
                 pltpu.VMEM((2, NP * rows, order), BF16),
                 pltpu.VMEM((2, order, order), F32),
                 pltpu.VMEM((2, order, order), BF16),
@@ -303,8 +346,18 @@
             compiler_params=pltpu.CompilerParams(
                 collective_id=0, has_side_effects=True, vmem_limit_bytes=24 * 2**20
             ),
-        )(grads, old_stat, counts)
-        return stat, out.reshape(NY * NX * NC * NP * 2, slab, order)
+        )(*(pltpu.with_memory_space_constraint(x, pltpu.HBM) for x in (grads, old_stat, counts)))
+        out = out.reshape(NY * NX * NC * NP * 2, slab, order)
+        anywhere = pl.BlockSpec(memory_space=pl.ANY)
+        return pl.pallas_call(
+            store,
+            out_shape=(pltpu.HBM(stat.shape, F32), pltpu.HBM(out.shape, BF16)),
+            in_specs=[pl.BlockSpec(memory_space=pltpu.VMEM)] * 2,
+            out_specs=(pl.BlockSpec(memory_space=pltpu.HBM),) * 2,
+            scratch_shapes=[pltpu.SemaphoreType.DMA((STORES + 1,))],
+            name="store_results",
+            compiler_params=pltpu.CompilerParams(vmem_limit_bytes=2**20),
+        )(*(pltpu.with_memory_space_constraint(x, pltpu.VMEM) for x in (stat, out)))
 
     return jax.shard_map(
         step,

time: 149 us -> 135 us (0.906)
  local copies, waits for them, and re-layouts: 11.9 us -> 0 us
  Pallas kernels: 136 us -> 133 us
    unnamed x8 -> x0, local copies, waits for them, and re-layouts: 11.9 us -> none
    pallas_call x1, Pallas kernels: 136 us -> 127 us  [step(): pl.pallas_call(kernel, out_shape=(pltpu.VMEM((2, order, order), F32), plt...]
    pallas_call x0 -> x1, Pallas kernels: none -> 6.56 us  [step(): pl.pallas_call(store, out_shape=(pltpu.HBM(stat.shape, F32), pltpu.HBM(ou...]
where the time goes in v2:
time: 135 us; the launch traced here: 134 us
  Pallas kernels  133 us (99%)
    pallas_call x1, Pallas kernels, step(): pl.pallas_call(kernel, out_shape=(pltpu.VMEM((2, order, order), F32), plt...  127 us
    pallas_call x1, Pallas kernels, step(): pl.pallas_call(store, out_shape=(pltpu.HBM(stat.shape, F32), pltpu.HBM(ou...  6.56 us

profile of v2, /device:TPU:3, one launch (start us, length us, event | category | flops | bytes accessed | tf_op | source)
XLA Modules:
  0.0 134.1 jit_solution(11308954304426221299)
XLA Ops:
  0.6 126.7 %shampoo_roots.1 = (f32[2,512,512]{2,1,0:T(8,128)S(1)}, bf16[16,8,2,64,512]{4,3,2,1,0:T(8,128)(2,1)S(1)}) custom-call(bf16[16,256,512]{2,1,0:T(8,128)(2,1)} %grads.1, f32[2,512,512]{2,1,0:T(8,128)} %old_hbm.1, s32[2]{0:T(128)} %counts_hbm.1), custom_call_target="tpu_custom_call" | custom-call | tf_op jit(solution)/shard_map/shampoo_roots/pallas_call | solution.py:324
  127.4 6.6 %store_results.1 = (f32[2,512,512]{2,1,0:T(8,128)}, bf16[256,64,512]{2,1,0:T(8,128)(2,1)}) custom-call(f32[2,512,512]{2,1,0:T(8,128)S(1)} %get-tuple-element.4.stat, bf16[256,64,512]{2,1,0:T(8,128)(2,1)S(1)} %bitcast.1), custom_call_target="tpu_custom_call" | custom-call | tf_op jit(solution)/shard_map/store_results/pallas_call | solution.py:352

commit v3 on v2

--- a/solution.py
+++ b/solution.py
@@ -16,10 +16,10 @@
 
 STORES = 8
 X, Y = "x", "y"
-MOST = ((X, "-"), (X, "+"), (X, "-"), (Y, "+"))
-HALF = ((X, "+"), (X, "-"), (Y, "+"), (Y, "-"))
-KINDS = (MOST, HALF)
-STOPS = (4, 12, 15, 18, 21, 24, 28)
+FULL = ((X, "+"), (X, "-"), (X, "+"), (X, "-"))
+HALF = ((Y, "+"), (X, "+"), (X, "-"), (Y, "-"))
+KINDS = (FULL, HALF)
+STOPS = (4, 10, 12, 14, 17, 20, 24)
 
 
 def ways_on(kind, dy, dx):

time: 135 us -> 128 us (0.948)
  Pallas kernels: 133 us -> 127 us
    pallas_call x1, Pallas kernels: 127 us -> 120 us  [step(): pl.pallas_call(kernel, out_shape=(pltpu.VMEM((2, order, order), F32), plt...]
where the time goes in v3:
time: 128 us; the launch traced here: 127 us
  Pallas kernels  127 us (99%)
    pallas_call x1, Pallas kernels, step(): pl.pallas_call(kernel, out_shape=(pltpu.VMEM((2, order, order), F32), plt...  120 us
    pallas_call x1, Pallas kernels, step(): pl.pallas_call(store, out_shape=(pltpu.HBM(stat.shape, F32), pltpu.HBM(ou...  6.56 us

profile of v3, /device:TPU:3, one launch (start us, length us, event | category | flops | bytes accessed | tf_op | source)
XLA Modules:
  0.0 127.4 jit_solution(680315533680971914)
XLA Ops:
  0.6 120.0 %shampoo_roots.1 = (f32[2,512,512]{2,1,0:T(8,128)S(1)}, bf16[16,8,2,64,512]{4,3,2,1,0:T(8,128)(2,1)S(1)}) custom-call(bf16[16,256,512]{2,1,0:T(8,128)(2,1)} %grads.1, f32[2,512,512]{2,1,0:T(8,128)} %old_hbm.1, s32[2]{0:T(128)} %counts_hbm.1), custom_call_target="tpu_custom_call" | custom-call | tf_op jit(solution)/shard_map/shampoo_roots/pallas_call | solution.py:324
  120.7 6.6 %store_results.1 = (f32[2,512,512]{2,1,0:T(8,128)}, bf16[256,64,512]{2,1,0:T(8,128)(2,1)}) custom-call(f32[2,512,512]{2,1,0:T(8,128)S(1)} %get-tuple-element.4.stat, bf16[256,64,512]{2,1,0:T(8,128)(2,1)S(1)} %bitcast.1), custom_call_target="tpu_custom_call" | custom-call | tf_op jit(solution)/shard_map/store_results/pallas_call | solution.py:352

commit v4 on v3

--- a/solution.py
+++ b/solution.py
@@ -19,7 +19,7 @@
 FULL = ((X, "+"), (X, "-"), (X, "+"), (X, "-"))
 HALF = ((Y, "+"), (X, "+"), (X, "-"), (Y, "-"))
 KINDS = (FULL, HALF)
-STOPS = (4, 10, 12, 14, 17, 20, 24)
+STOPS = (4, 10, 12, 14, 16, 18, 20)
 
 
 def ways_on(kind, dy, dx):
@@ -206,9 +206,11 @@
             device_id_type=MESH,
         ).wait_recv()
 
-    def spread(j):
+    def spread(j, meanwhile=0):
         for p in range(1, NP):
             slab_copies[j][p].start()
+        if meanwhile:
+            relay(0, meanwhile, len(relays[0]))
         out[dp, mp, j] = root[j, pl.ds(pl.multiple_of(mp * slab, slab), slab), :]
         for t in range(NP // 2):
             for p in (2 * t, 2 * t + 1):
@@ -276,8 +278,7 @@
         step_m()
     relay(0, STOPS[ITERS - 1], STOPS[ITERS])
     finish(1)
-    spread(1)
-    relay(0, STOPS[ITERS], len(relays[0]))
+    spread(1, STOPS[ITERS])
     relay(1, 0, len(relays[1]))
 
     for j in range(2):

time: 128 us -> 129 us (level)
  no operation moved by 1% of the time
where the time goes in v4:
time: 129 us; the launch traced here: 128 us
  Pallas kernels  127 us (98%)
    pallas_call x1, Pallas kernels, step(): pl.pallas_call(kernel, out_shape=(pltpu.VMEM((2, order, order), F32), plt...  121 us
    pallas_call x1, Pallas kernels, step(): pl.pallas_call(store, out_shape=(pltpu.HBM(stat.shape, F32), pltpu.HBM(ou...  6.56 us

profile of v4, /device:TPU:3, one launch (start us, length us, event | category | flops | bytes accessed | tf_op | source)
XLA Modules:
  0.0 128.3 jit_solution(4809745692435856912)
XLA Ops:
  0.6 120.9 %shampoo_roots.1 = (f32[2,512,512]{2,1,0:T(8,128)S(1)}, bf16[16,8,2,64,512]{4,3,2,1,0:T(8,128)(2,1)S(1)}) custom-call(bf16[16,256,512]{2,1,0:T(8,128)(2,1)} %grads.1, f32[2,512,512]{2,1,0:T(8,128)} %old_hbm.1, s32[2]{0:T(128)} %counts_hbm.1), custom_call_target="tpu_custom_call" | custom-call | tf_op jit(solution)/shard_map/shampoo_roots/pallas_call | solution.py:325
  121.5 6.6 %store_results.1 = (f32[2,512,512]{2,1,0:T(8,128)}, bf16[256,64,512]{2,1,0:T(8,128)(2,1)}) custom-call(f32[2,512,512]{2,1,0:T(8,128)S(1)} %get-tuple-element.4.stat, bf16[256,64,512]{2,1,0:T(8,128)(2,1)S(1)} %bitcast.1), custom_call_target="tpu_custom_call" | custom-call | tf_op jit(solution)/shard_map/store_results/pallas_call | solution.py:353
